TPU v7x, 256 devices: a whole 4x4x8 slice. The times are simulated.
256 devices in a mesh: rep: 16 (over x, z_hi, core), fsdp: 16 (over y, z_lo).
Axes of the slice: x: 4, y: 4, z: 8 (z_hi: 2, z_lo: 4; z = z_hi * 4 + z_lo), core: 2. Of those that a mesh axis runs over, the one named last changes fastest.
Arguments:
- tokens: bfloat16 [16, 4096, 4608], P('rep', 'fsdp'), may hold values from -240 to 240
- gain_offset: float32 [16, 4608], P('rep'), may hold values from -1.5 to 1.5
- key_weight: bfloat16 [16, 4608, 1024], P('rep', 'fsdp'), may hold values from -0.09375 to 0.09375
- key_cotangent: bfloat16 [16, 4096, 1024], P('rep', 'fsdp'), may hold values from -6 to 6
- outer_fragment: float32 [4608, 1024], P('fsdp'), may hold values from -6 to 6
- outer_momentum: float32 [4608, 1024], P('fsdp'), may hold values from -3 to 3
- inner_fragment: bfloat16 [16, 4608, 1024], P('rep', 'fsdp'), may hold values from -6 to 6
Outputs:
- input_grad: bfloat16 [16, 4096, 4608], P('rep', 'fsdp')
- gain_grad: float32 [16, 4608], P('rep')
- weight_grad: float32 [16, 4608, 1024], P('rep', 'fsdp')
- new_outer: float32 [4608, 1024], P('fsdp')
- new_momentum: float32 [4608, 1024], P('fsdp')
All inputs are finite; a program needn't handle non-finite values.
Results may differ from a plain program's by a relative error of at most 0.012.
Values may be sent and summed in bfloat16 or wider, within the bound.
A program may use at most 128 MiB of HBM per device.

v0:
```python
import jax
import jax.numpy as jnp
from jax import lax
from jax.sharding import PartitionSpec as P

EPSILON = 1e-06
OUTER_RATE = 0.7
MOMENTUM = 0.9


def nesterov(outer_part, momentum_part, summed, replicas):
    pseudo = summed / replicas
    momentum_next = MOMENTUM * momentum_part + pseudo
    return (outer_part - OUTER_RATE * (pseudo + MOMENTUM * momentum_next), momentum_next)


def local(
    tokens, gain_offset, key_weight, key_cotangent, outer_fragment, outer_momentum, inner_fragment
):
    source = tokens[0].astype(jnp.float32)
    inverse = lax.rsqrt(jnp.mean(source * source, axis=1, keepdims=True) + EPSILON)
    unit = source * inverse
    factor = 1.0 + gain_offset[0]
    normed = (unit * factor).astype(jnp.bfloat16)
    upstream = key_cotangent[0]
    weight = key_weight[0]
    product = lax.dot_general(
        upstream,
        lax.all_gather(weight, "fsdp", axis=0, tiled=True),
        (((1,), (1,)), ((), ())),
        preferred_element_type=jnp.float32,
    )
    feature_grad = product.astype(jnp.bfloat16)
    weight_grad = lax.psum_scatter(
        lax.dot_general(
            normed, upstream, (((0,), (0,)), ((), ())), preferred_element_type=jnp.float32
        ),
        "fsdp",
        scatter_dimension=0,
        tiled=True,
    )
    grad_float = feature_grad.astype(jnp.float32)
    gain_grad = lax.psum(jnp.sum(grad_float * unit, axis=0), "fsdp")
    scaled = grad_float * factor
    projected = jnp.mean(scaled * unit, axis=1, keepdims=True)
    input_grad = (inverse * (scaled - unit * projected)).astype(jnp.bfloat16)
    replicas = lax.axis_size("rep")
    differences = outer_fragment - inner_fragment[0].astype(jnp.float32)
    summed = lax.psum(differences, "rep")
    new_outer, new_momentum = nesterov(outer_fragment, outer_momentum, summed, replicas)
    return (input_grad[None], gain_grad[None], weight_grad[None], new_outer, new_momentum)


def solution(mesh):
    return jax.shard_map(
        local,
        mesh=mesh,
        in_specs=(
            P("rep", "fsdp", None),
            P("rep", None),
            P("rep", "fsdp", None),
            P("rep", "fsdp", None),
            P("fsdp", None),
            P("fsdp", None),
            P("rep", "fsdp", None),
        ),
        out_specs=(
            P("rep", "fsdp", None),
            P("rep", None),
            P("rep", "fsdp", None),
            P("fsdp", None),
            P("fsdp", None),
        ),
        check_vma=False,
    )
```

profile of v0, /device:TPU:0, one launch (start us, length us, event | category | flops | bytes accessed | tf_op | source)
XLA Modules:
  0.0 737.3 jit_solution(7853563532229758204)
XLA Ops:
  8.0 0.0 copy-start
  8.0 0.0 copy-start.2
  8.0 0.0 copy-start.1
  8.0 0.0 all-reduce.2.cloned.1.call-start
  8.1 2.8 convert_subtract_fusion
  10.9 0.0 all-reduce.2.cloned.1.call-update
  10.9 0.0 all-gather.3.cloned.1.call-start
  10.9 0.5 all-gather.3.cloned.1.call-update
  11.5 0.0 reduce-scatter.2.cloned.1.call-start
  11.5 0.0 copy-done.2
  11.5 0.1 add_reduce_fusion
  11.6 0.0 copy-done.1
  11.6 0.5 fusion.18
  12.2 0.0 copy-done
  12.2 8.0 %fusion.22 = f32[4608,1024]{1,0:T(8,128)} fusion(bf16[1,256,4608]{2,1,0:T(8,128)(2,1)S(1)} %copy-done.1, f32[4608]{0:T(1024)S(1)} %add_reduce_fusion, f32[256]{0:T(256)S(1)} %add_rsqrt_fusion, bf16[1,256,1024]{2,1,0:T(8,128)(2,1)S(1)} %copy-done), kind=kOutput, calls=%fused_computation.20 | convolution fusion | flops 2420637696 | bytes 21777408 | tf_op jit(solution)/shard_map/dot_general | solution.py:35
  20.2 0.0 reduce-scatter.2.cloned.1.call-update
  20.2 599.6 %all-reduce.2.cloned.1.call-done = f32[288,1024]{1,0:T(8,128)} async-done(((f32[288,1024]{1,0:T(8,128)}), f32[288,1024]{1,0:T(8,128)}) %all-reduce.2.cloned.1.call-update) | async-done | bytes 1179664 | tf_op jit(solution)/shard_map/psum | solution.py:49
  619.8 4.0 multiply_subtract_fusion
  623.8 0.0 all-gather.3.cloned.1.call-done
  623.8 9.2 %fusion.17 = (f32[4608]{0:T(1024)S(1)}, f32[256]{0:T(256)S(1)}, f32[256,4608]{1,0:T(8,128)}) fusion(bf16[1,256,4608]{2,1,0:T(8,128)(2,1)S(1)} %copy-done.1, f32[256]{0:T(256)S(1)} %add_rsqrt_fusion, f32[4608]{0:T(1024)S(1)} %add_reduce_fusion, bf16[1,4608,1024]{2,1,0:T(8,128)(2,1)} %all-gather.3.cloned.1.call-done, bf16[1,256,1024]{2,1,0:T(8,128)(2,1)S(1)} %copy-done), kind=kOutput, calls=%fused_computation.15 | convolution fusion | flops 2426531072 | bytes 17078272 | tf_op jit(solution)/shard_map/dot_general | solution.py:27
  633.1 91.8 %psum.14 = f32[1,4608]{1,0:T(1,128)} all-reduce(f32[1,4608]{1,0:T(1,128)S(1)} %broadcast_in_dim.14), channel_id=1, replica_groups=mesh['rep'=16,'fsdp'=16] {'fsdp'}, use_global_device_ids=true, to_apply=%region_3.0 | all-reduce | flops 4608 | bytes 36864 | tf_op jit(solution)/shard_map/psum | solution.py:43
  724.9 5.0 fusion.24
  729.9 0.0 reduce-scatter.2.cloned.1.call-done
  (3 shorter events, 0.0 us)
Async XLA Ops:
  8.0 4.2 copy-start
  8.0 3.5 copy-start.2
  8.0 3.6 copy-start.1
  8.0 611.8 %all-reduce.2.cloned.1.call-start = ((), (), s32[]{:S(2)}) async-start(), calls=%async_computation.2 | async-start | bytes 2359296 | tf_op jit(solution)/shard_map/psum | solution.py:49
  10.9 613.0 %all-gather.3.cloned.1.call-start = ((), (), s32[]{:S(2)}) async-start(), calls=%async_computation.3 | async-start | bytes 10027008 | tf_op jit(solution)/shard_map/all_gather | solution.py:29
  11.5 718.4 %reduce-scatter.2.cloned.1.call-start = ((), (), s32[]{:S(2)}) async-start(), calls=%async_computation.1 | async-start | bytes 20054016 | tf_op jit(solution)/shard_map/reduce_scatter | solution.py:34
Sparse Core Ops, SparseCore 0:
  12.1 607.7 all-reduce.1
Sparse Core Ops, SparseCore 1:
  13.1 231.4 all-gather.2
  247.6 419.2 reduce-scatter.1
where the time goes:
time: 738 us; the launch traced here: 737 us
  waiting for transfers between devices  600 us (81%)
  blocking collectives  91.8 us (12%)
  matrix products  17.2 us (2%)
  between operations  15.5 us (2%)
  other arithmetic  12.4 us (2%)
    psum x1, waiting for transfers between devices, local(): summed = lax.psum(differences, 'rep')  600 us
    psum x1, blocking collectives, local(): gain_grad = lax.psum(jnp.sum(grad_float * unit, axis=0), 'fsdp')  91.8 us
  transfers between devices with their start and end apart: 3, of which 1 were waited for; matrix products, arithmetic and copies ran while one was open for 4% of the time, Pallas kernels for 0%

commit v1 on v0

v1 whole, which is shorter than its diff:
```python
import jax
import jax.numpy as jnp
from jax import lax
from jax.experimental import pallas as pl
from jax.experimental.pallas import tpu as pltpu
from jax.sharding import PartitionSpec as P

EPSILON = 1e-06
OUTER_RATE = 0.7
MOMENTUM = 0.9

MESH = pl.DeviceIdType.MESH
F32 = jnp.float32
BF16 = jnp.bfloat16

D = 4608
KW = 1024
ROWS = 256
SHARD = 288
BLOCK = 1152
CHUNK = 384
NCHUNK = 3
REPS = 16
PIECES = 4
PIECE = ROWS // PIECES
LANE = 128

WITH_FSDP = True
WITH_REP = True


def kernel(
    tokens,
    gain,
    weight,
    cotangent,
    outer,
    momentum,
    inner,
    input_grad,
    gain_grad,
    weight_grad,
    new_outer,
    new_momentum,
    tok_v,
    gain_v,
    cx,
    wx,
    tx,
    rs_own,
    rsx,
    rb,
    nt,
    gp,
    sb,
    ru,
    rd,
    wg_v,
    fx,
    fin,
    ig_v,
    gz,
    gy,
    gg_v,
    outer_v,
    mom_v,
    inner_v,
    db,
    cr,
    s1,
    xr,
    zs,
    zr,
    xs,
    no_v,
    nm_v,
    loc,
    tok_loc,
    out_sem,
    c_s,
    c_r,
    t_s,
    t_r,
    r_s,
    r_r,
    w_s,
    w_f,
    w_r,
    g_s,
    u_r,
    d_r,
    f_s,
    f_r,
    gz_s,
    gz_r,
    gy_s,
    gy_r,
    k_s,
    k_r,
    x_s,
    x_r,
    h_s,
    h_r,
):
    fi = lax.axis_index("fsdp")
    ri = lax.axis_index("rep")
    y, z = fi // 4, lax.rem(fi, 4)
    x, zh, core = ri // 4, lax.rem(ri // 2, 2), lax.rem(ri, 2)

    def y_peer(d):
        return (ri, lax.rem(y + d, 4) * 4 + z)

    def z_peer(to):
        return (ri, y * 4 + to)

    def x_peer(d):
        return (lax.rem(x + d, 4) * 4 + zh * 2 + core, fi)

    h_peer = (x * 4 + (1 - zh) * 2 + core, fi)
    core_peer = (x * 4 + zh * 2 + (1 - core), fi)

    def remote(src, dst, send, recv, peer):
        return pltpu.make_async_remote_copy(
            src_ref=src, dst_ref=dst, send_sem=send, recv_sem=recv, device_id=peer, device_id_type=MESH
        )

    def local(src, dst, sem):
        copy = pltpu.make_async_copy(src, dst, sem)
        copy.start()
        return copy

    def chunk_at(step):
        return jnp.where(z < 2, NCHUNK - 1 - step, step)

    def chunk_columns(block, chunk):
        return pl.ds(pl.multiple_of(block * BLOCK + chunk * CHUNK, LANE), CHUNK)

    def shard_rows(j):
        return pl.ds(pl.multiple_of(j * SHARD, 32), SHARD)

    copies = {}
    if WITH_FSDP:
        copies["tokens"] = local(tokens.at[0], tok_v, loc.at[0])
        copies["gain"] = local(gain, gain_v, loc.at[1])
        copies["c"] = local(cotangent.at[0], cx.at[y], loc.at[2])
        copies["w"] = local(weight.at[0], wx.at[shard_rows(z)], loc.at[3])
        for step in range(NCHUNK):
            chunk = chunk_at(step)
            copies["t", step] = local(
                tokens.at[0, :, chunk_columns(y, chunk)], tx.at[chunk, y], tok_loc.at[step]
            )
    if WITH_REP:
        copies["outer"] = local(outer, outer_v, loc.at[4])
        copies["momentum"] = local(momentum, mom_v, loc.at[5])
        copies["inner"] = local(inner.at[0], inner_v, loc.at[6])

    barrier = pltpu.get_barrier_semaphore()
    peers = []
    if WITH_FSDP:
        peers += [y_peer(d) for d in (1, 2, 3)] + [z_peer(lax.rem(z + d, 4)) for d in (1, 2, 3)]
    if WITH_REP:
        peers += [x_peer(d) for d in (1, 2, 3)] + [h_peer, core_peer]
    for peer in peers:
        pl.semaphore_signal(barrier, inc=1, device_id=peer, device_id_type=MESH)
    pl.semaphore_wait(barrier, len(peers))

    sends = []

    def start(copy):
        copy.start()
        sends.append(copy)
        return copy

    def c_copy(i):
        if i == 0:
            return remote(cotangent.at[0], cx.at[y], c_s.at[0], c_r.at[0], y_peer(1))
        if i == 1:
            return remote(cotangent.at[0], cx.at[y], c_s.at[1], c_r.at[1], y_peer(3))
        if i == 2:
            half = cx.at[lax.rem(y + 3, 4), pl.ds(0, ROWS // 2)]
            return remote(half, half, c_s.at[2], c_r.at[2], y_peer(1))
        half = cx.at[lax.rem(y + 1, 4), pl.ds(ROWS // 2, ROWS // 2)]
        return remote(half, half, c_s.at[3], c_r.at[3], y_peer(3))

    def t_copy(step, d):
        chunk = chunk_at(step)
        return remote(
            tokens.at[0, :, chunk_columns(lax.rem(y + d, 4), chunk)],
            tx.at[chunk, y],
            t_s.at[step, d - 1],
            t_r.at[step, d - 1],
            y_peer(d),
        )

    def start_tokens(step):
        for d in (1, 3, 2):
            start(t_copy(step, d))

    def r_copy(d):
        return remote(rsx.at[y], rsx.at[y], r_s.at[d - 1], r_r.at[d - 1], y_peer(d))

    up, down = jnp.minimum(z + 1, 3), jnp.maximum(z - 1, 0)

    def w_own(i):
        to = up if i == 0 else down
        return remote(weight.at[0], wx.at[shard_rows(z)], w_s.at[i], w_r.at[z], z_peer(to))

    def w_forward(j, to):
        rows = wx.at[shard_rows(j)]
        return remote(rows, rows, w_f.at[j], w_r.at[j], z_peer(to))

    def weight_step(s):
        @pl.when(z >= s)
        def _():
            w_forward(z - s, up).wait_recv()

            @pl.when(z < 3)
            def _():
                w_forward(z - s, up).start()

        @pl.when(z + s <= 3)
        def _():
            w_forward(z + s, down).wait_recv()

            @pl.when(z > 0)
            def _():
                w_forward(z + s, down).start()

    def g_up(j):
        return remote(sb.at[j], ru.at[j], g_s.at[j], u_r.at[j], z_peer(up))

    def g_down(j):
        return remote(sb.at[j], rd.at[j], g_s.at[j], d_r.at[j], z_peer(down))

    def send_sum(j, arrived, copy, first):
        def add(i, _):
            rows = pl.ds(pl.multiple_of(i * 32, 32), 32)
            part = gp[pl.ds(pl.multiple_of(j * SHARD + i * 32, 32), 32), :]
            if not first:
                part = part + arrived[j, rows, :].astype(F32)
            sb[j, rows, :] = part.astype(BF16)
            return 0

        if not first:
            copy(j).wait_recv()
        lax.fori_loop(0, SHARD // 32, add, 0)
        copy(j).start()

    def sums_up(j, first):
        send_sum(j, ru, g_up, first)

    def sums_down(j, first):
        send_sum(j, rd, g_down, first)

    def sum_step(s):
        if s == 1:

            @pl.when(z == 0)
            def _():
                sums_up(3, True)

            @pl.when(z == 3)
            def _():
                sums_down(0, True)
        elif s == 2:

            @pl.when(z == 0)
            def _():
                sums_up(2, True)

            @pl.when(z == 3)
            def _():
                sums_down(1, True)

            @pl.when(z == 1)
            def _():
                sums_up(3, False)

            @pl.when(z == 2)
            def _():
                sums_down(0, False)
        else:

            @pl.when(z == 0)
            def _():
                sums_up(1, True)

            @pl.when(z == 3)
            def _():
                sums_down(2, True)

            @pl.when(z == 1)
            def _():
                sums_up(2, False)
                sums_down(0, False)

            @pl.when(z == 2)
            def _():
                sums_down(1, False)
                sums_up(3, False)

    def sum_last():
        @pl.when(z > 0)
        def _():
            g_up(z).wait_recv()

        @pl.when(z < 3)
        def _():
            g_down(z).wait_recv()

        def add(i, _):
            rows = pl.ds(pl.multiple_of(i * 32, 32), 32)
            wg_v[rows, :] = gp[pl.ds(pl.multiple_of(z * SHARD + i * 32, 32), 32), :]

            @pl.when(z > 0)
            def _():
                wg_v[rows, :] += ru[z, rows, :].astype(F32)

            @pl.when(z < 3)
            def _():
                wg_v[rows, :] += rd[z, rows, :].astype(F32)

            return 0

        lax.fori_loop(0, SHARD // 32, add, 0)
        copies["weight_grad"] = local(wg_v, weight_grad.at[0], out_sem.at[0])

    def f_copy(piece, d):
        to = lax.rem(y + d, 4)
        rows = pl.ds(piece * PIECE, PIECE)
        return remote(
            fx.at[:, to, rows],
            fin.at[y, :, rows],
            f_s.at[piece, d - 1],
            f_r.at[piece, d - 1],
            y_peer(d),
        )

    def start_features(piece):
        for d in (1, 3, 2):
            start(f_copy(piece, d))

    def gz_copy(d):
        return remote(gz.at[z], gz.at[z], gz_s.at[d - 1], gz_r.at[d - 1], z_peer(lax.rem(z + d, 4)))

    def gy_copy(d):
        return remote(gy.at[y], gy.at[y], gy_s.at[d - 1], gy_r.at[d - 1], y_peer(d))

    def k_copy(i):
        if i == 0:
            return remote(db.at[pl.ds((1 - core) * 4, 4)], cr, k_s.at[0], k_r.at[0], core_peer)
        part = xs.at[pl.ds(core * 4, 4)]
        return remote(part, part, k_s.at[1], k_r.at[1], core_peer)

    def x_copy(i, d):
        if i == 0:
            return remote(
                s1.at[lax.rem(x + d, 4)], xr.at[d - 1], x_s.at[0, d - 1], x_r.at[0, d - 1], x_peer(d)
            )
        part = xs.at[core * 4 + x]
        return remote(part, part, x_s.at[1, d - 1], x_r.at[1, d - 1], x_peer(d))

    def h_copy():
        return remote(zs, zr, h_s, h_r, h_peer)

    def inverse_root():
        def body(i, _):
            rows = pl.ds(pl.multiple_of(i * 16, 16), 16)
            total = jnp.zeros((16, LANE), F32)
            for j in range(D // LANE):
                v = tok_v[rows, j * LANE : (j + 1) * LANE].astype(F32)
                total = total + v * v
            mean = jnp.sum(total, axis=1, keepdims=True) / D
            rs_own[rows, :] = jnp.broadcast_to(lax.rsqrt(mean + EPSILON), (16, LANE))
            return 0

        lax.fori_loop(0, ROWS // 16, body, 0)
        rsx[y] = jnp.transpose(rs_own[...])[0:8, :]

    def spread_roots():
        def body(s, _):
            rb[s] = jnp.transpose(jnp.broadcast_to(rsx[s][0:1, :], (LANE, ROWS)))
            return 0

        lax.fori_loop(0, 4, body, 0)

    def weight_chunk(chunk):
        def norm(s, _):
            for q in range(CHUNK // LANE):
                unit = tx[chunk, s, :, q * LANE : (q + 1) * LANE].astype(F32) * rb[s]
                at = pl.multiple_of(y * BLOCK + chunk * CHUNK + q * LANE, LANE)
                normed = (unit * (1.0 + gain_v[0:1, pl.ds(at, LANE)])).astype(BF16)
                nt[s, q * LANE : (q + 1) * LANE, :] = jnp.transpose(normed)
            return 0

        lax.fori_loop(0, 4, norm, 0)

        def multiply(j, _):
            columns = pl.ds(pl.multiple_of(j * 256, 256), 256)
            total = jnp.zeros((CHUNK, 256), F32)
            for s in range(4):
                total = total + jnp.dot(nt[s], cx[s, :, columns], preferred_element_type=F32)
            gp[pl.ds(pl.multiple_of(chunk * CHUNK, CHUNK), CHUNK), columns] = total
            return 0

        lax.fori_loop(0, KW // 256, multiply, 0)

    def features():
        def body(i, _):
            t, s = i // 4, lax.rem(i, 4)
            product = lax.dot_general(
                cx[s],
                wx[pl.ds(pl.multiple_of(t * CHUNK, CHUNK), CHUNK), :],
                (((1,), (1,)), ((), ())),
                preferred_element_type=F32,
            )
            fx[t, s] = product.astype(BF16)
            return 0

        lax.fori_loop(0, NCHUNK * 4, body, 0)

    def gain_part():
        gz[z] = jnp.zeros((16, LANE), F32)

        def body(t, _):
            for q in range(CHUNK // LANE):
                lanes = slice(q * LANE, (q + 1) * LANE)

                def add(s, total):
                    unit = tx[t, s, :, lanes].astype(F32) * rb[s]
                    term = fx[t, s, :, lanes].astype(F32) * unit
                    return total + jnp.sum(term.reshape(ROWS // 8, 8, LANE), axis=0)

                total = lax.fori_loop(0, 4, add, jnp.zeros((8, LANE), F32))
                gz[z, pl.ds(t * (CHUNK // LANE) + q, 1), :] = jnp.sum(total, axis=0, keepdims=True)
            return 0

        lax.fori_loop(0, NCHUNK, body, 0)

    def input_piece(piece):
        def body(i, _):
            rows = pl.ds(pl.multiple_of(piece * PIECE + i * 16, 16), 16)
            root = rs_own[rows, :]

            def terms(s, t, q):
                at = s * BLOCK + t * CHUNK + q * LANE
                grad = fin[s, t, rows, q * LANE : (q + 1) * LANE].astype(F32)
                unit = tok_v[rows, at : at + LANE].astype(F32) * root
                return at, grad * (1.0 + gain_v[0:1, at : at + LANE]), unit

            places = [(s, t, q) for s in range(4) for t in range(NCHUNK) for q in range(CHUNK // LANE)]
            total = jnp.zeros((16, LANE), F32)
            for place in places:
                _, scaled, unit = terms(*place)
                total = total + scaled * unit
            projected = jnp.sum(total, axis=1, keepdims=True) / D
            for place in places:
                at, scaled, unit = terms(*place)
                ig_v[rows, at : at + LANE] = (root * (scaled - unit * projected)).astype(BF16)
            return 0

        lax.fori_loop(0, PIECE // 16, body, 0)
        rows = pl.ds(piece * PIECE, PIECE)
        copies["ig", piece] = local(ig_v.at[rows], input_grad.at[0, rows], out_sem.at[1 + piece])

    if WITH_FSDP:
        start(c_copy(0))
        start(c_copy(1))

        @pl.when(z < 3)
        def _():
            w_own(0).start()

        @pl.when(z > 0)
        def _():
            w_own(1).start()

        start_tokens(0)

    if WITH_REP:
        copies["outer"].wait()
        copies["inner"].wait()
        for b in range(8):
            lanes = slice(b * LANE, (b + 1) * LANE)
            db[b] = outer_v[:, lanes] - inner_v[:, lanes].astype(F32)
        start(k_copy(0))

    if WITH_FSDP:
        copies["tokens"].wait()
        inverse_root()
        for d in (1, 2, 3):
            start(r_copy(d))

    if WITH_REP:
        k_copy(0).wait_recv()
        for q in range(4):
            s1[q] = db[core * 4 + q] + cr[q]
        for d in (1, 2, 3):
            start(x_copy(0, d))
        for d in (1, 2, 3):
            x_copy(0, d).wait_recv()
        zs[...] = (s1[x] + xr[0] + xr[1] + xr[2]).astype(BF16)
        start(h_copy())

    if WITH_FSDP:
        c_copy(0).wait_recv()
        c_copy(1).wait_recv()
        start(c_copy(2))
        start(c_copy(3))
        start_tokens(1)
        weight_step(1)

    if WITH_REP:
        h_copy().wait_recv()
        xs[core * 4 + x] = zs[...].astype(F32) + zr[...].astype(F32)
        for d in (1, 2, 3):
            start(x_copy(1, d))
        for d in (1, 2, 3):
            x_copy(1, d).wait_recv()
        start(k_copy(1))

    if WITH_FSDP:
        copies["gain"].wait()
        for d in (1, 2, 3):
            r_copy(d).wait_recv()
        spread_roots()
        copies["c"].wait()
        copies["t", 0].wait()
        for d in (1, 2, 3):
            t_copy(0, d).wait_recv()
        start_tokens(2)
        c_copy(2).wait_recv()
        c_copy(3).wait_recv()
        weight_chunk(chunk_at(0))
        sum_step(1)
        weight_step(2)

    if WITH_REP:
        copies["momentum"].wait()
        k_copy(1).wait_recv()
        for b in range(8):
            lanes = slice(b * LANE, (b + 1) * LANE)
            pseudo = xs[b] / REPS
            momentum_next = MOMENTUM * mom_v[:, lanes] + pseudo
            nm_v[:, lanes] = momentum_next
            no_v[:, lanes] = outer_v[:, lanes] - OUTER_RATE * (pseudo + MOMENTUM * momentum_next)
        copies["new_outer"] = local(no_v, new_outer, out_sem.at[5])
        copies["new_momentum"] = local(nm_v, new_momentum, out_sem.at[6])

    if WITH_FSDP:
        copies["t", 1].wait()
        for d in (1, 2, 3):
            t_copy(1, d).wait_recv()
        weight_chunk(chunk_at(1))
        copies["w"].wait()
        weight_step(3)
        features()
        start_features(0)
        start_features(1)
        own = local(fx.at[:, y], fin.at[y], loc.at[7])
        sum_step(2)
        copies["t", 2].wait()
        for d in (1, 2, 3):
            t_copy(2, d).wait_recv()
        weight_chunk(chunk_at(2))
        gain_part()
        for d in (1, 2, 3):
            start(gz_copy(d))
        own.wait()
        for piece in range(PIECES):
            for d in (1, 2, 3):
                f_copy(piece, d).wait_recv()
            if piece + 2 < PIECES:
                start_features(piece + 2)
            input_piece(piece)
            if piece == 0:
                for d in (1, 2, 3):
                    gz_copy(d).wait_recv()
                gy[y] = gz[0] + gz[1] + gz[2] + gz[3]
                for d in (1, 2, 3):
                    start(gy_copy(d))
                sum_step(3)
            if piece == 1:
                for d in (1, 2, 3):
                    gy_copy(d).wait_recv()
                for b in range(4):
                    for i in range(BLOCK // LANE):
                        at = b * BLOCK + i * LANE
                        gg_v[0:1, at : at + LANE] = gy[b, i : i + 1, :]
                copies["gain_grad"] = local(gg_v, gain_grad, out_sem.at[7])
            if piece == 2:
                sum_last()

    for copy in sends:
        copy.wait_send()
    if WITH_FSDP:

        @pl.when(z < 3)
        def _():
            w_own(0).wait_send()

        @pl.when(z > 0)
        def _():
            w_own(1).wait_send()

        for s in (1, 2):

            @pl.when((z >= s) & (z < 3))
            def _():
                w_forward(z - s, up).wait_send()

            @pl.when((z + s <= 3) & (z > 0))
            def _():
                w_forward(z + s, down).wait_send()

        for d in (1, 2, 3):
            g_up(lax.rem(z + d, 4)).wait_send()
        copies["weight_grad"].wait()
        copies["gain_grad"].wait()
        for piece in range(PIECES):
            copies["ig", piece].wait()
    if WITH_REP:
        copies["new_outer"].wait()
        copies["new_momentum"].wait()


def call(*args):
    shapes = (
        jax.ShapeDtypeStruct((1, ROWS, D), BF16),
        jax.ShapeDtypeStruct((1, D), F32),
        jax.ShapeDtypeStruct((1, SHARD, KW), F32),
        jax.ShapeDtypeStruct((SHARD, KW), F32),
        jax.ShapeDtypeStruct((SHARD, KW), F32),
    )
    dma = pltpu.SemaphoreType.DMA
    scratch = [
        pltpu.VMEM((ROWS, D), BF16),
        pltpu.VMEM((1, D), F32),
        pltpu.VMEM((4, ROWS, KW), BF16),
        pltpu.VMEM((BLOCK, KW), BF16),
        pltpu.VMEM((NCHUNK, 4, ROWS, CHUNK), BF16),
        pltpu.VMEM((ROWS, LANE), F32),
        pltpu.VMEM((4, 8, ROWS), F32),
        pltpu.VMEM((4, ROWS, LANE), F32),
        pltpu.VMEM((4, CHUNK, ROWS), BF16),
        pltpu.VMEM((BLOCK, KW), F32),
        pltpu.VMEM((4, SHARD, KW), BF16),
        pltpu.VMEM((4, SHARD, KW), BF16),
        pltpu.VMEM((4, SHARD, KW), BF16),
        pltpu.VMEM((SHARD, KW), F32),
        pltpu.VMEM((NCHUNK, 4, ROWS, CHUNK), BF16),
        pltpu.VMEM((4, NCHUNK, ROWS, CHUNK), BF16),
        pltpu.VMEM((ROWS, D), BF16),
        pltpu.VMEM((4, 16, LANE), F32),
        pltpu.VMEM((4, 16, LANE), F32),
        pltpu.VMEM((1, D), F32),
        pltpu.VMEM((SHARD, KW), F32),
        pltpu.VMEM((SHARD, KW), F32),
        pltpu.VMEM((SHARD, KW), BF16),
        pltpu.VMEM((8, SHARD, LANE), F32),
        pltpu.VMEM((4, SHARD, LANE), F32),
        pltpu.VMEM((4, SHARD, LANE), F32),
        pltpu.VMEM((3, SHARD, LANE), F32),
        pltpu.VMEM((SHARD, LANE), BF16),
        pltpu.VMEM((SHARD, LANE), BF16),
        pltpu.VMEM((8, SHARD, LANE), F32),
        pltpu.VMEM((SHARD, KW), F32),
        pltpu.VMEM((SHARD, KW), F32),
        dma((8,)),
        dma((NCHUNK,)),
        dma((8,)),
        dma((4,)),
        dma((4,)),
        dma((NCHUNK, 3)),
        dma((NCHUNK, 3)),
        dma((3,)),
        dma((3,)),
        dma((2,)),
        dma((4,)),
        dma((4,)),
        dma((4,)),
        dma((4,)),
        dma((4,)),
        dma((PIECES, 3)),
        dma((PIECES, 3)),
        dma((3,)),
        dma((3,)),
        dma((3,)),
        dma((3,)),
        dma((2,)),
        dma((2,)),
        dma((2, 3)),
        dma((2, 3)),
        dma,
        dma,
    ]
    anywhere = pl.BlockSpec(memory_space=pl.ANY)
    return pl.pallas_call(
        kernel,
        out_shape=shapes,
        in_specs=[anywhere] * 7,
        out_specs=[anywhere] * 5,
        scratch_shapes=scratch,
        compiler_params=pltpu.CompilerParams(
            collective_id=0, has_side_effects=True, vmem_limit_bytes=60 * 2**20
        ),
        cost_estimate=pl.CostEstimate(
            flops=4 * ROWS * D * KW, bytes_accessed=16 * 2**20, transcendentals=ROWS
        ),
        name="inner_outer_step",
    )(*args)


def solution(mesh):
    return jax.shard_map(
        call,
        mesh=mesh,
        in_specs=(
            P("rep", "fsdp", None),
            P("rep", None),
            P("rep", "fsdp", None),
            P("rep", "fsdp", None),
            P("fsdp", None),
            P("fsdp", None),
            P("rep", "fsdp", None),
        ),
        out_specs=(
            P("rep", "fsdp", None),
            P("rep", None),
            P("rep", "fsdp", None),
            P("fsdp", None),
            P("fsdp", None),
        ),
        check_vma=False,
    )
```

time: 738 us -> 97.6 us (0.13)
  the two profiles are of different devices: /device:TPU:0 before, /device:TPU:6 now
where the time goes in v1:
time: 97.6 us; the launch traced here: 95.9 us
  Pallas kernels  86.9 us (89%)
  local copies, waits for them, and re-layouts  8.34 us (9%)
    pallas_call x1, Pallas kernels, call(): pl.pallas_call(kernel, out_shape=shapes, in_specs=[anywhere] * 7, out_spe...  86.9 us
    unnamed x13, local copies, waits for them, and re-layouts  8.34 us

profile of v1, /device:TPU:6, one launch (start us, length us, event | category | flops | bytes accessed | tf_op | source)
XLA Modules:
  0.0 95.9 jit_solution(6233416169454201757)
XLA Ops:
  0.6 86.9 %inner_outer_step.1 = (bf16[1,256,4608]{2,1,0:T(8,128)(2,1)}, f32[1,4608]{1,0:T(1,128)}, f32[1,288,1024]{2,1,0:T(8,128)}, f32[288,1024]{1,0:T(8,128)}, f32[288,1024]{1,0:T(8,128)}) custom-call(bf16[1,256,4608]{2,1,0:T(8,128)(2,1)} %tokens.1, f32[1,4608]{1,0:T(1,128)} %gain.1, bf16[1,288,1024]{2,1,0:T(8,128)(2,1)} %weight.1, bf16[1,256,1024]{2,1,0:T(8,128)(2,1)} %cotangent.1, ...), custom_call_target="tpu_custom_call" | custom-call | flops 4831838208 | bytes 16777216 | tf_op jit(solution)/shard_map/inner_outer_step/pallas_call | solution.py:698
  87.5 0.0 copy-start.3
  87.5 0.0 copy-start.2
  87.5 3.3 %copy.17 = bf16[1,256,4608]{2,1,0:T(8,128)(2,1)} copy(bf16[1,256,4608]{2,1,0:T(8,128)(2,1)} %get-tuple-element.10) | data formatting | bytes 4718592
  90.9 0.0 copy-done.3
  90.9 0.6 copy.18
  91.5 0.0 copy-done.2
  91.5 0.0 copy-start.1
  91.5 1.0 %copy.19 = f32[1,288,1024]{2,1,0:T(8,128)} copy(f32[1,288,1024]{2,1,0:T(8,128)S(1)} %copy-done.2) | data formatting | bytes 2359296
  92.5 0.7 copy-done.1
  93.2 0.0 copy-start
  93.2 1.0 %copy.20 = f32[288,1024]{1,0:T(8,128)} copy(f32[288,1024]{1,0:T(8,128)S(1)} %copy-done.1) | data formatting | bytes 2359296
  94.2 0.7 copy-done
  94.9 1.0 %copy.21 = f32[288,1024]{1,0:T(8,128)} copy(f32[288,1024]{1,0:T(8,128)S(1)} %copy-done) | data formatting | bytes 2359296
Async XLA Ops:
  87.5 3.3 %copy-start.3 = (f32[1,4608]{1,0:T(1,128)S(1)}, f32[1,4608]{1,0:T(1,128)}, u32[]{:S(2)}) copy-start(f32[1,4608]{1,0:T(1,128)} %get-tuple-element.11) | copy-start | bytes 55300
  87.5 3.9 %copy-start.2 = (f32[1,288,1024]{2,1,0:T(8,128)S(1)}, f32[1,288,1024]{2,1,0:T(8,128)}, u32[]{:S(2)}) copy-start(f32[1,288,1024]{2,1,0:T(8,128)} %get-tuple-element.12) | copy-start | bytes 3538948
  91.5 1.7 %copy-start.1 = (f32[288,1024]{1,0:T(8,128)S(1)}, f32[288,1024]{1,0:T(8,128)}, u32[]{:S(2)}) copy-start(f32[288,1024]{1,0:T(8,128)} %get-tuple-element.13) | copy-start | bytes 3538948
  93.2 1.7 %copy-start = (f32[288,1024]{1,0:T(8,128)S(1)}, f32[288,1024]{1,0:T(8,128)}, u32[]{:S(2)}) copy-start(f32[288,1024]{1,0:T(8,128)} %get-tuple-element.14) | copy-start | bytes 3538948

commit v2 on v1

--- a/solution.py
+++ b/solution.py
@@ -23,7 +23,10 @@
 REPS = 16
 PIECES = 4
 PIECE = ROWS // PIECES
+HALF = ROWS // 2
+PART = SHARD // 2
 LANE = 128
+VMEM_LIMIT = 48 * 2**20
 
 WITH_FSDP = True
 WITH_REP = True
@@ -37,11 +40,11 @@
     outer,
     momentum,
     inner,
-    input_grad,
-    gain_grad,
-    weight_grad,
-    new_outer,
-    new_momentum,
+    ig_v,
+    gg_v,
+    wg_v,
+    no_v,
+    nm_v,
     tok_v,
     gain_v,
     cx,
@@ -55,13 +58,10 @@
     sb,
     ru,
     rd,
-    wg_v,
     fx,
     fin,
-    ig_v,
     gz,
     gy,
-    gg_v,
     outer_v,
     mom_v,
     inner_v,
@@ -72,11 +72,8 @@
     zs,
     zr,
     xs,
-    no_v,
-    nm_v,
     loc,
     tok_loc,
-    out_sem,
     c_s,
     c_r,
     t_s,
@@ -91,6 +88,8 @@
     d_r,
     f_s,
     f_r,
+    p_s,
+    p_r,
     gz_s,
     gz_r,
     gy_s,
@@ -141,17 +140,8 @@
     copies = {}
     if WITH_FSDP:
         copies["tokens"] = local(tokens.at[0], tok_v, loc.at[0])
-        copies["gain"] = local(gain, gain_v, loc.at[1])
-        copies["c"] = local(cotangent.at[0], cx.at[y], loc.at[2])
-        copies["w"] = local(weight.at[0], wx.at[shard_rows(z)], loc.at[3])
-        for step in range(NCHUNK):
-            chunk = chunk_at(step)
-            copies["t", step] = local(
-                tokens.at[0, :, chunk_columns(y, chunk)], tx.at[chunk, y], tok_loc.at[step]
-            )
     if WITH_REP:
         copies["outer"] = local(outer, outer_v, loc.at[4])
-        copies["momentum"] = local(momentum, mom_v, loc.at[5])
         copies["inner"] = local(inner.at[0], inner_v, loc.at[6])
 
     barrier = pltpu.get_barrier_semaphore()
@@ -172,15 +162,16 @@
         return copy
 
     def c_copy(i):
-        if i == 0:
-            return remote(cotangent.at[0], cx.at[y], c_s.at[0], c_r.at[0], y_peer(1))
-        if i == 1:
-            return remote(cotangent.at[0], cx.at[y], c_s.at[1], c_r.at[1], y_peer(3))
-        if i == 2:
-            half = cx.at[lax.rem(y + 3, 4), pl.ds(0, ROWS // 2)]
-            return remote(half, half, c_s.at[2], c_r.at[2], y_peer(1))
-        half = cx.at[lax.rem(y + 1, 4), pl.ds(ROWS // 2, ROWS // 2)]
-        return remote(half, half, c_s.at[3], c_r.at[3], y_peer(3))
+        first, second = pl.ds(0, HALF), pl.ds(HALF, HALF)
+        if i < 4:
+            rows = first if i in (0, 3) else second
+            at = cx.at[y, rows]
+            return remote(cotangent.at[0, rows], at, c_s.at[i], c_r.at[i], y_peer(1 if i in (0, 2) else 3))
+        if i == 4:
+            part = cx.at[lax.rem(y + 3, 4), first]
+            return remote(part, part, c_s.at[4], c_r.at[4], y_peer(1))
+        part = cx.at[lax.rem(y + 1, 4), second]
+        return remote(part, part, c_s.at[5], c_r.at[5], y_peer(3))
 
     def t_copy(step, d):
         chunk = chunk_at(step)
@@ -192,10 +183,6 @@
             y_peer(d),
         )
 
-    def start_tokens(step):
-        for d in (1, 3, 2):
-            start(t_copy(step, d))
-
     def r_copy(d):
         return remote(rsx.at[y], rsx.at[y], r_s.at[d - 1], r_r.at[d - 1], y_peer(d))
 
@@ -226,119 +213,89 @@
             def _():
                 w_forward(z + s, down).start()
 
-    def g_up(j):
-        return remote(sb.at[j], ru.at[j], g_s.at[j], u_r.at[j], z_peer(up))
-
-    def g_down(j):
-        return remote(sb.at[j], rd.at[j], g_s.at[j], d_r.at[j], z_peer(down))
-
-    def send_sum(j, arrived, copy, first):
+    def g_up(j, part):
+        at = (j, pl.ds(part * PART, PART))
+        return remote(sb.at[at], ru.at[at], g_s.at[j, part], u_r.at[j, part], z_peer(up))
+
+    def g_down(j, part):
+        at = (j, pl.ds(part * PART, PART))
+        return remote(sb.at[at], rd.at[at], g_s.at[j, part], d_r.at[j, part], z_peer(down))
+
+    def send_sum(j, part, arrived, copy, first):
         def add(i, _):
-            rows = pl.ds(pl.multiple_of(i * 32, 32), 32)
-            part = gp[pl.ds(pl.multiple_of(j * SHARD + i * 32, 32), 32), :]
+            at = part * PART + i * 16
+            rows = pl.ds(pl.multiple_of(at, 16), 16)
+            total = gp[pl.ds(pl.multiple_of(j * SHARD + at, 16), 16), :]
             if not first:
-                part = part + arrived[j, rows, :].astype(F32)
-            sb[j, rows, :] = part.astype(BF16)
+                total = total + arrived[j, rows, :].astype(F32)
+            sb[j, rows, :] = total.astype(BF16)
             return 0
 
         if not first:
-            copy(j).wait_recv()
-        lax.fori_loop(0, SHARD // 32, add, 0)
-        copy(j).start()
-
-    def sums_up(j, first):
-        send_sum(j, ru, g_up, first)
-
-    def sums_down(j, first):
-        send_sum(j, rd, g_down, first)
-
-    def sum_step(s):
-        if s == 1:
-
-            @pl.when(z == 0)
+            copy(j, part).wait_recv()
+        lax.fori_loop(0, PART // 16, add, 0)
+        copy(j, part).start()
+
+    def begin_sums(step):
+        @pl.when(z == 0)
+        def _():
+            for part in range(2):
+                send_sum(3 - step, part, ru, g_up, True)
+
+        @pl.when(z == 3)
+        def _():
+            for part in range(2):
+                send_sum(step, part, rd, g_down, True)
+
+    def pass_sums(step, part):
+        routes = (((3, ru, g_up), (0, rd, g_down)), ((0, rd, g_down), (3, ru, g_up)), ((2, ru, g_up), (1, rd, g_down)))
+        for at, (j, arrived, copy) in zip((1, 2), routes[step]):
+
+            @pl.when(z == at)
             def _():
-                sums_up(3, True)
-
-            @pl.when(z == 3)
-            def _():
-                sums_down(0, True)
-        elif s == 2:
-
-            @pl.when(z == 0)
-            def _():
-                sums_up(2, True)
-
-            @pl.when(z == 3)
-            def _():
-                sums_down(1, True)
-
-            @pl.when(z == 1)
-            def _():
-                sums_up(3, False)
-
-            @pl.when(z == 2)
-            def _():
-                sums_down(0, False)
-        else:
-
-            @pl.when(z == 0)
-            def _():
-                sums_up(1, True)
-
-            @pl.when(z == 3)
-            def _():
-                sums_down(2, True)
-
-            @pl.when(z == 1)
-            def _():
-                sums_up(2, False)
-                sums_down(0, False)
-
-            @pl.when(z == 2)
-            def _():
-                sums_down(1, False)
-                sums_up(3, False)
-
-    def sum_last():
+                send_sum(j, part, arrived, copy, False)
+
+    def end_sums(part):
         @pl.when(z > 0)
         def _():
-            g_up(z).wait_recv()
+            g_up(z, part).wait_recv()
 
         @pl.when(z < 3)
         def _():
-            g_down(z).wait_recv()
+            g_down(z, part).wait_recv()
 
         def add(i, _):
-            rows = pl.ds(pl.multiple_of(i * 32, 32), 32)
-            wg_v[rows, :] = gp[pl.ds(pl.multiple_of(z * SHARD + i * 32, 32), 32), :]
+            at = part * PART + i * 16
+            rows = pl.ds(pl.multiple_of(at, 16), 16)
+            wg_v[0, rows, :] = gp[pl.ds(pl.multiple_of(z * SHARD + at, 16), 16), :]
 
             @pl.when(z > 0)
             def _():
-                wg_v[rows, :] += ru[z, rows, :].astype(F32)
+                wg_v[0, rows, :] += ru[z, rows, :].astype(F32)
 
             @pl.when(z < 3)
             def _():
-                wg_v[rows, :] += rd[z, rows, :].astype(F32)
+                wg_v[0, rows, :] += rd[z, rows, :].astype(F32)
 
             return 0
 
-        lax.fori_loop(0, SHARD // 32, add, 0)
-        copies["weight_grad"] = local(wg_v, weight_grad.at[0], out_sem.at[0])
-
-    def f_copy(piece, d):
+        lax.fori_loop(0, PART // 16, add, 0)
+
+    def feature_chunk(step):
+        return jnp.where(z < 2, step, NCHUNK - 1 - step)
+
+    def f_copy(step, d):
+        chunk = feature_chunk(step)
+        to = lax.rem(y + d, 4)
+        return remote(fx.at[chunk, to], fin.at[y, chunk], f_s.at[step, d - 1], f_r.at[step, d - 1], y_peer(d))
+
+    def p_copy(piece, d):
+        chunk = feature_chunk(NCHUNK - 1)
         to = lax.rem(y + d, 4)
         rows = pl.ds(piece * PIECE, PIECE)
         return remote(
-            fx.at[:, to, rows],
-            fin.at[y, :, rows],
-            f_s.at[piece, d - 1],
-            f_r.at[piece, d - 1],
-            y_peer(d),
+            fx.at[chunk, to, rows], fin.at[y, chunk, rows], p_s.at[piece, d - 1], p_r.at[piece, d - 1], y_peer(d)
         )
-
-    def start_features(piece):
-        for d in (1, 3, 2):
-            start(f_copy(piece, d))
 
     def gz_copy(d):
         return remote(gz.at[z], gz.at[z], gz_s.at[d - 1], gz_r.at[d - 1], z_peer(lax.rem(z + d, 4)))
@@ -405,19 +362,15 @@
 
         lax.fori_loop(0, KW // 256, multiply, 0)
 
-    def features():
-        def body(i, _):
-            t, s = i // 4, lax.rem(i, 4)
-            product = lax.dot_general(
-                cx[s],
-                wx[pl.ds(pl.multiple_of(t * CHUNK, CHUNK), CHUNK), :],
-                (((1,), (1,)), ((), ())),
-                preferred_element_type=F32,
-            )
-            fx[t, s] = product.astype(BF16)
-            return 0
-
-        lax.fori_loop(0, NCHUNK * 4, body, 0)
+    def features(step):
+        chunk = feature_chunk(step)
+        product = lax.dot_general(
+            cx[...].reshape(4 * ROWS, KW),
+            wx[pl.ds(pl.multiple_of(chunk * CHUNK, CHUNK), CHUNK), :],
+            (((1,), (1,)), ((), ())),
+            preferred_element_type=F32,
+        )
+        fx[chunk] = product.astype(BF16).reshape(4, ROWS, CHUNK)
 
     def gain_part():
         gz[z] = jnp.zeros((16, LANE), F32)
@@ -456,16 +409,14 @@
             projected = jnp.sum(total, axis=1, keepdims=True) / D
             for place in places:
                 at, scaled, unit = terms(*place)
-                ig_v[rows, at : at + LANE] = (root * (scaled - unit * projected)).astype(BF16)
+                ig_v[0, rows, at : at + LANE] = (root * (scaled - unit * projected)).astype(BF16)
             return 0
 
         lax.fori_loop(0, PIECE // 16, body, 0)
-        rows = pl.ds(piece * PIECE, PIECE)
-        copies["ig", piece] = local(ig_v.at[rows], input_grad.at[0, rows], out_sem.at[1 + piece])
-
-    if WITH_FSDP:
-        start(c_copy(0))
-        start(c_copy(1))
+
+    if WITH_FSDP:
+        for i in range(4):
+            start(c_copy(i))
 
         @pl.when(z < 3)
         def _():
@@ -475,7 +426,16 @@
         def _():
             w_own(1).start()
 
-        start_tokens(0)
+        copies["gain"] = local(gain, gain_v, loc.at[1])
+        copies["c"] = local(cotangent.at[0], cx.at[y], loc.at[2])
+        copies["w"] = local(weight.at[0], wx.at[shard_rows(z)], loc.at[3])
+        for step in range(NCHUNK):
+            chunk = chunk_at(step)
+            copies["t", step] = local(
+                tokens.at[0, :, chunk_columns(y, chunk)], tx.at[chunk, y], tok_loc.at[step]
+            )
+    if WITH_REP:
+        copies["momentum"] = local(momentum, mom_v, loc.at[5])
 
     if WITH_REP:
         copies["outer"].wait()
@@ -488,8 +448,15 @@
     if WITH_FSDP:
         copies["tokens"].wait()
         inverse_root()
-        for d in (1, 2, 3):
+        for d in (1, 3, 2):
             start(r_copy(d))
+        c_copy(0).wait_recv()
+        start(c_copy(4))
+        c_copy(1).wait_recv()
+        start(c_copy(5))
+        for step in range(NCHUNK):
+            for d in (1, 3, 2):
+                start(t_copy(step, d))
 
     if WITH_REP:
         k_copy(0).wait_recv()
@@ -497,43 +464,61 @@
             s1[q] = db[core * 4 + q] + cr[q]
         for d in (1, 2, 3):
             start(x_copy(0, d))
+
+    if WITH_FSDP:
+        weight_step(1)
+
+    if WITH_REP:
         for d in (1, 2, 3):
             x_copy(0, d).wait_recv()
         zs[...] = (s1[x] + xr[0] + xr[1] + xr[2]).astype(BF16)
         start(h_copy())
 
     if WITH_FSDP:
-        c_copy(0).wait_recv()
-        c_copy(1).wait_recv()
-        start(c_copy(2))
-        start(c_copy(3))
-        start_tokens(1)
-        weight_step(1)
-
-    if WITH_REP:
-        h_copy().wait_recv()
-        xs[core * 4 + x] = zs[...].astype(F32) + zr[...].astype(F32)
-        for d in (1, 2, 3):
-            start(x_copy(1, d))
-        for d in (1, 2, 3):
-            x_copy(1, d).wait_recv()
-        start(k_copy(1))
-
-    if WITH_FSDP:
         copies["gain"].wait()
         for d in (1, 2, 3):
             r_copy(d).wait_recv()
         spread_roots()
         copies["c"].wait()
+        for i in range(2, 6):
+            c_copy(i).wait_recv()
         copies["t", 0].wait()
         for d in (1, 2, 3):
             t_copy(0, d).wait_recv()
-        start_tokens(2)
-        c_copy(2).wait_recv()
-        c_copy(3).wait_recv()
         weight_chunk(chunk_at(0))
-        sum_step(1)
+        begin_sums(0)
+        copies["w"].wait()
         weight_step(2)
+        for step in range(NCHUNK - 1):
+            features(step)
+            for d in (1, 3, 2):
+                start(f_copy(step, d))
+
+    if WITH_REP:
+        h_copy().wait_recv()
+        xs[core * 4 + x] = zs[...].astype(F32) + zr[...].astype(F32)
+        for d in (1, 2, 3):
+            start(x_copy(1, d))
+
+    if WITH_FSDP:
+        copies["t", 1].wait()
+        for d in (1, 2, 3):
+            t_copy(1, d).wait_recv()
+        weight_chunk(chunk_at(1))
+        begin_sums(1)
+        pass_sums(0, 0)
+
+    if WITH_REP:
+        for d in (1, 2, 3):
+            x_copy(1, d).wait_recv()
+        start(k_copy(1))
+
+    if WITH_FSDP:
+        weight_step(3)
+        features(NCHUNK - 1)
+        for piece in range(PIECES - 1):
+            for d in (1, 3, 2):
+                start(p_copy(piece, d))
 
     if WITH_REP:
         copies["momentum"].wait()
@@ -544,52 +529,47 @@
             momentum_next = MOMENTUM * mom_v[:, lanes] + pseudo
             nm_v[:, lanes] = momentum_next
             no_v[:, lanes] = outer_v[:, lanes] - OUTER_RATE * (pseudo + MOMENTUM * momentum_next)
-        copies["new_outer"] = local(no_v, new_outer, out_sem.at[5])
-        copies["new_momentum"] = local(nm_v, new_momentum, out_sem.at[6])
-
-    if WITH_FSDP:
-        copies["t", 1].wait()
-        for d in (1, 2, 3):
-            t_copy(1, d).wait_recv()
-        weight_chunk(chunk_at(1))
-        copies["w"].wait()
-        weight_step(3)
-        features()
-        start_features(0)
-        start_features(1)
+
+    if WITH_FSDP:
         own = local(fx.at[:, y], fin.at[y], loc.at[7])
-        sum_step(2)
+        pass_sums(0, 1)
         copies["t", 2].wait()
         for d in (1, 2, 3):
             t_copy(2, d).wait_recv()
+        gain_part()
+        for d in (1, 2, 3):
+            start(gz_copy(d))
         weight_chunk(chunk_at(2))
-        gain_part()
-        for d in (1, 2, 3):
-            start(gz_copy(d))
+        begin_sums(2)
+        pass_sums(1, 0)
+        pass_sums(2, 0)
+        pass_sums(1, 1)
+        for d in (1, 2, 3):
+            gz_copy(d).wait_recv()
+        gy[y] = gz[0] + gz[1] + gz[2] + gz[3]
+        for d in (1, 3, 2):
+            start(gy_copy(d))
+        for d in (1, 3, 2):
+            start(p_copy(PIECES - 1, d))
+        pass_sums(2, 1)
         own.wait()
+        for step in range(NCHUNK - 1):
+            for d in (1, 2, 3):
+                f_copy(step, d).wait_recv()
         for piece in range(PIECES):
-            for d in (1, 2, 3):
-                f_copy(piece, d).wait_recv()
-            if piece + 2 < PIECES:
-                start_features(piece + 2)
-            input_piece(piece)
-            if piece == 0:
-                for d in (1, 2, 3):
-                    gz_copy(d).wait_recv()
-                gy[y] = gz[0] + gz[1] + gz[2] + gz[3]
-                for d in (1, 2, 3):
-                    start(gy_copy(d))
-                sum_step(3)
             if piece == 1:
+                end_sums(0)
+            if piece == PIECES - 1:
+                end_sums(1)
                 for d in (1, 2, 3):
                     gy_copy(d).wait_recv()
                 for b in range(4):
                     for i in range(BLOCK // LANE):
                         at = b * BLOCK + i * LANE
                         gg_v[0:1, at : at + LANE] = gy[b, i : i + 1, :]
-                copies["gain_grad"] = local(gg_v, gain_grad, out_sem.at[7])
-            if piece == 2:
-                sum_last()
+            for d in (1, 2, 3):
+                p_copy(piece, d).wait_recv()
+            input_piece(piece)
 
     for copy in sends:
         copy.wait_send()
@@ -614,17 +594,24 @@
                 w_forward(z + s, down).wait_send()
 
         for d in (1, 2, 3):
-            g_up(lax.rem(z + d, 4)).wait_send()
-        copies["weight_grad"].wait()
-        copies["gain_grad"].wait()
-        for piece in range(PIECES):
-            copies["ig", piece].wait()
-    if WITH_REP:
-        copies["new_outer"].wait()
-        copies["new_momentum"].wait()
-
-
-def call(*args):
+            for part in range(2):
+                g_up(lax.rem(z + d, 4), part).wait_send()
+
+
+def finish(*refs):
+    sources, targets, sems = refs[:5], refs[5:10], refs[10]
+    copies = [
+        pltpu.make_async_copy(source, target, sems.at[i])
+        for i, (source, target) in enumerate(zip(sources, targets))
+    ]
+    for copy in copies:
+        copy.start()
+    for copy in copies:
+        copy.wait()
+
+
+def call(tokens, gain, *rest):
+    args = (tokens, pltpu.with_memory_space_constraint(gain, pltpu.HBM), *rest)
     shapes = (
         jax.ShapeDtypeStruct((1, ROWS, D), BF16),
         jax.ShapeDtypeStruct((1, D), F32),
@@ -647,13 +634,10 @@
         pltpu.VMEM((4, SHARD, KW), BF16),
         pltpu.VMEM((4, SHARD, KW), BF16),
         pltpu.VMEM((4, SHARD, KW), BF16),
-        pltpu.VMEM((SHARD, KW), F32),
         pltpu.VMEM((NCHUNK, 4, ROWS, CHUNK), BF16),
         pltpu.VMEM((4, NCHUNK, ROWS, CHUNK), BF16),
-        pltpu.VMEM((ROWS, D), BF16),
         pltpu.VMEM((4, 16, LANE), F32),
         pltpu.VMEM((4, 16, LANE), F32),
-        pltpu.VMEM((1, D), F32),
         pltpu.VMEM((SHARD, KW), F32),
         pltpu.VMEM((SHARD, KW), F32),
         pltpu.VMEM((SHARD, KW), BF16),
@@ -664,13 +648,10 @@
         pltpu.VMEM((SHARD, LANE), BF16),
         pltpu.VMEM((SHARD, LANE), BF16),
         pltpu.VMEM((8, SHARD, LANE), F32),
-        pltpu.VMEM((SHARD, KW), F32),
-        pltpu.VMEM((SHARD, KW), F32),
         dma((8,)),
         dma((NCHUNK,)),
-        dma((8,)),
-        dma((4,)),
-        dma((4,)),
+        dma((6,)),
+        dma((6,)),
         dma((NCHUNK, 3)),
         dma((NCHUNK, 3)),
         dma((3,)),
@@ -678,9 +659,11 @@
         dma((2,)),
         dma((4,)),
         dma((4,)),
-        dma((4,)),
-        dma((4,)),
-        dma((4,)),
+        dma((4, 2)),
+        dma((4, 2)),
+        dma((4, 2)),
+        dma((NCHUNK - 1, 3)),
+        dma((NCHUNK - 1, 3)),
         dma((PIECES, 3)),
         dma((PIECES, 3)),
         dma((3,)),
@@ -694,21 +677,31 @@
         dma,
         dma,
     ]
-    anywhere = pl.BlockSpec(memory_space=pl.ANY)
-    return pl.pallas_call(
+    anywhere = pl.BlockSpec(memory_space=pltpu.HBM)
+    on_chip = pl.BlockSpec(memory_space=pltpu.VMEM)
+    results = pl.pallas_call(
         kernel,
-        out_shape=shapes,
+        out_shape=tuple(pltpu.VMEM(shape.shape, shape.dtype) for shape in shapes),
         in_specs=[anywhere] * 7,
-        out_specs=[anywhere] * 5,
+        out_specs=[on_chip] * 5,
         scratch_shapes=scratch,
         compiler_params=pltpu.CompilerParams(
-            collective_id=0, has_side_effects=True, vmem_limit_bytes=60 * 2**20
+            collective_id=0, has_side_effects=True, vmem_limit_bytes=VMEM_LIMIT
         ),
         cost_estimate=pl.CostEstimate(
             flops=4 * ROWS * D * KW, bytes_accessed=16 * 2**20, transcendentals=ROWS
         ),
         name="inner_outer_step",
     )(*args)
+    return pl.pallas_call(
+        finish,
+        out_shape=shapes,
+        in_specs=[on_chip] * 5,
+        out_specs=[anywhere] * 5,
+        scratch_shapes=[pltpu.SemaphoreType.DMA((5,))],
+        compiler_params=pltpu.CompilerParams(vmem_limit_bytes=2**20),
+        name="write_results",
+    )(*(pltpu.with_memory_space_constraint(result, pltpu.VMEM) for result in results))
 
 
 def solution(mesh):

time: 97.6 us -> 85.1 us (0.87); the launches traced: 95.9 us -> 85 us
  local copies, waits for them, and re-layouts: 8.34 us -> 0 us
  Pallas kernels: 86.9 us -> 84.4 us
    unnamed x13 -> x0, local copies, waits for them, and re-layouts: 8.34 us -> none
    pallas_call x1 -> x2, Pallas kernels: 86.9 us -> 84.4 us  [the longest x1 81.8 us: call(): pl.pallas_call(kernel, out_shape=tuple((pltpu.VMEM(shape.shape, shape.dty...]
where the time goes in v2:
time: 85.1 us; the launch traced here: 85 us
  Pallas kernels  84.4 us (99%)
    pallas_call x1, Pallas kernels, call(): pl.pallas_call(kernel, out_shape=tuple((pltpu.VMEM(shape.shape, shape.dty...  81.8 us
    pallas_call x1, Pallas kernels, call(): pl.pallas_call(finish, out_shape=shapes, in_specs=[on_chip] * 5, out_spec...  2.62 us

profile of v2, /device:TPU:6, one launch (start us, length us, event | category | flops | bytes accessed | tf_op | source)
XLA Modules:
  0.0 85.0 jit_solution(9033218002415401657)
XLA Ops:
  0.6 81.8 %inner_outer_step.1 = (bf16[1,256,4608]{2,1,0:T(8,128)(2,1)S(1)}, f32[1,4608]{1,0:T(1,128)S(1)}, f32[1,288,1024]{2,1,0:T(8,128)S(1)}, f32[288,1024]{1,0:T(8,128)S(1)}, f32[288,1024]{1,0:T(8,128)S(1)}) custom-call(bf16[1,256,4608]{2,1,0:T(8,128)(2,1)} %tokens.1, f32[1,4608]{1,0:T(1,128)} %gain.1, bf16[1,288,1024]{2,1,0:T(8,128)(2,1)} %weight.1, ...), custom_call_target="tpu_custom_call" | custom-call | flops 4831838208 | bytes 16777216 | tf_op jit(solution)/shard_map/inner_outer_step/pallas_call | solution.py:682
  82.4 2.6 %write_results.1 = (bf16[1,256,4608]{2,1,0:T(8,128)(2,1)}, f32[1,4608]{1,0:T(1,128)}, f32[1,288,1024]{2,1,0:T(8,128)}, f32[288,1024]{1,0:T(8,128)}, f32[288,1024]{1,0:T(8,128)}) custom-call(bf16[1,256,4608]{2,1,0:T(8,128)(2,1)S(1)} %get-tuple-element.10.refs_0_, f32[1,4608]{1,0:T(1,128)S(1)} %get-tuple-element.11.refs_1_, ...), custom_call_target="tpu_custom_call" | custom-call | tf_op jit(solution)/shard_map/write_results/pallas_call | solution.py:696

commit v3 on v2

--- a/solution.py
+++ b/solution.py
@@ -72,6 +72,11 @@
     zs,
     zr,
     xs,
+    near_z,
+    far_z,
+    all_x,
+    one_h,
+    one_core,
     loc,
     tok_loc,
     c_s,
@@ -145,14 +150,69 @@
         copies["inner"] = local(inner.at[0], inner_v, loc.at[6])
 
     barrier = pltpu.get_barrier_semaphore()
-    peers = []
-    if WITH_FSDP:
-        peers += [y_peer(d) for d in (1, 2, 3)] + [z_peer(lax.rem(z + d, 4)) for d in (1, 2, 3)]
+    expected = 0
+
+    def arrive(peer):
+        pl.semaphore_signal(barrier, inc=1, device_id=peer, device_id_type=MESH)
+
+    def answer(sem, peer):
+        pl.semaphore_signal(sem, inc=1, device_id=peer, device_id_type=MESH)
+
+    if WITH_FSDP:
+        for d in (1, 2, 3):
+            arrive(y_peer(d))
+        for d in (1, 2, 3):
+
+            @pl.when(z + d <= 3)
+            def _():
+                arrive(z_peer(lax.rem(z + d, 4)))
+
+        expected = expected + 3 + z
     if WITH_REP:
-        peers += [x_peer(d) for d in (1, 2, 3)] + [h_peer, core_peer]
-    for peer in peers:
-        pl.semaphore_signal(barrier, inc=1, device_id=peer, device_id_type=MESH)
-    pl.semaphore_wait(barrier, len(peers))
+        for d in (1, 2, 3):
+
+            @pl.when(x + d <= 3)
+            def _():
+                arrive(x_peer(d))
+
+        @pl.when(zh == 0)
+        def _():
+            arrive(h_peer)
+
+        @pl.when(core == 1)
+        def _():
+            arrive(core_peer)
+
+        expected = expected + x + zh + (1 - core)
+    pl.semaphore_wait(barrier, expected)
+
+    def answers():
+        if WITH_FSDP:
+
+            @pl.when(z >= 1)
+            def _():
+                answer(near_z, z_peer(jnp.maximum(z - 1, 0)))
+
+            for d in (2, 3):
+
+                @pl.when(z >= d)
+                def _():
+                    answer(far_z, z_peer(jnp.maximum(z - d, 0)))
+
+        if WITH_REP:
+            for d in (1, 2, 3):
+
+                @pl.when(x >= d)
+                def _():
+                    answer(all_x, x_peer(4 - d))
+
+            @pl.when(zh == 1)
+            def _():
+                answer(one_h, h_peer)
+
+            @pl.when(core == 0)
+            def _():
+                answer(one_core, core_peer)
 
     sends = []
 
@@ -418,13 +478,11 @@
         for i in range(4):
             start(c_copy(i))
 
-        @pl.when(z < 3)
-        def _():
-            w_own(0).start()
-
         @pl.when(z > 0)
         def _():
             w_own(1).start()
+
+        answers()
 
         copies["gain"] = local(gain, gain_v, loc.at[1])
         copies["c"] = local(cotangent.at[0], cx.at[y], loc.at[2])
@@ -436,6 +494,14 @@
             )
     if WITH_REP:
         copies["momentum"] = local(momentum, mom_v, loc.at[5])
+    if not WITH_FSDP:
+        answers()
+    if WITH_FSDP:
+
+        @pl.when(z < 3)
+        def _():
+            pl.semaphore_wait(near_z, 1)
+            w_own(0).start()
 
     if WITH_REP:
         copies["outer"].wait()
@@ -443,6 +509,11 @@
         for b in range(8):
             lanes = slice(b * LANE, (b + 1) * LANE)
             db[b] = outer_v[:, lanes] - inner_v[:, lanes].astype(F32)
+
+        @pl.when(core == 1)
+        def _():
+            pl.semaphore_wait(one_core, 1)
+
         start(k_copy(0))
 
     if WITH_FSDP:
@@ -462,6 +533,11 @@
         k_copy(0).wait_recv()
         for q in range(4):
             s1[q] = db[core * 4 + q] + cr[q]
+
+        @pl.when(x < 3)
+        def _():
+            pl.semaphore_wait(all_x, 3 - x)
+
         for d in (1, 2, 3):
             start(x_copy(0, d))
 
@@ -472,6 +548,11 @@
         for d in (1, 2, 3):
             x_copy(0, d).wait_recv()
         zs[...] = (s1[x] + xr[0] + xr[1] + xr[2]).astype(BF16)
+
+        @pl.when(zh == 0)
+        def _():
+            pl.semaphore_wait(one_h, 1)
+
         start(h_copy())
 
     if WITH_FSDP:
@@ -537,6 +618,11 @@
         for d in (1, 2, 3):
             t_copy(2, d).wait_recv()
         gain_part()
+
+        @pl.when(z < 2)
+        def _():
+            pl.semaphore_wait(far_z, 2 - z)
+
         for d in (1, 2, 3):
             start(gz_copy(d))
         weight_chunk(chunk_at(2))
@@ -648,6 +734,11 @@
         pltpu.VMEM((SHARD, LANE), BF16),
         pltpu.VMEM((SHARD, LANE), BF16),
         pltpu.VMEM((8, SHARD, LANE), F32),
+        pltpu.SemaphoreType.REGULAR,
+        pltpu.SemaphoreType.REGULAR,
+        pltpu.SemaphoreType.REGULAR,
+        pltpu.SemaphoreType.REGULAR,
+        pltpu.SemaphoreType.REGULAR,
         dma((8,)),
         dma((NCHUNK,)),
         dma((6,)),

time: 85.1 us -> 80.8 us (0.949); the launches traced: 85 us -> 79.3 us
  Pallas kernels: 84.4 us -> 78.6 us
    pallas_call x1, Pallas kernels: 81.8 us -> 76 us  [call(): pl.pallas_call(kernel, out_shape=tuple((pltpu.VMEM(shape.shape, shape.dty...]
where the time goes in v3:
time: 80.8 us; the launch traced here: 79.3 us
  Pallas kernels  78.6 us (97%)
    pallas_call x1, Pallas kernels, call(): pl.pallas_call(kernel, out_shape=tuple((pltpu.VMEM(shape.shape, shape.dty...  76 us
    pallas_call x1, Pallas kernels, call(): pl.pallas_call(finish, out_shape=shapes, in_specs=[on_chip] * 5, out_spec...  2.62 us

profile of v3, /device:TPU:6, one launch (start us, length us, event | category | flops | bytes accessed | tf_op | source)
XLA Modules:
  0.0 79.3 jit_solution(3702386765988179279)
XLA Ops:
  0.6 76.0 %inner_outer_step.1 = (bf16[1,256,4608]{2,1,0:T(8,128)(2,1)S(1)}, f32[1,4608]{1,0:T(1,128)S(1)}, f32[1,288,1024]{2,1,0:T(8,128)S(1)}, f32[288,1024]{1,0:T(8,128)S(1)}, f32[288,1024]{1,0:T(8,128)S(1)}) custom-call(bf16[1,256,4608]{2,1,0:T(8,128)(2,1)} %tokens.1, f32[1,4608]{1,0:T(1,128)} %gain.1, bf16[1,288,1024]{2,1,0:T(8,128)(2,1)} %weight.1, ...), custom_call_target="tpu_custom_call" | custom-call | flops 4831838208 | bytes 16777216 | tf_op jit(solution)/shard_map/inner_outer_step/pallas_call | solution.py:773
  76.7 2.6 %write_results.1 = (bf16[1,256,4608]{2,1,0:T(8,128)(2,1)}, f32[1,4608]{1,0:T(1,128)}, f32[1,288,1024]{2,1,0:T(8,128)}, f32[288,1024]{1,0:T(8,128)}, f32[288,1024]{1,0:T(8,128)}) custom-call(bf16[1,256,4608]{2,1,0:T(8,128)(2,1)S(1)} %get-tuple-element.10.refs_0_, f32[1,4608]{1,0:T(1,128)S(1)} %get-tuple-element.11.refs_1_, ...), custom_call_target="tpu_custom_call" | custom-call | tf_op jit(solution)/shard_map/write_results/pallas_call | solution.py:787

commit v4 on v3

--- a/solution.py
+++ b/solution.py
@@ -21,7 +21,7 @@
 CHUNK = 384
 NCHUNK = 3
 REPS = 16
-PIECES = 4
+PIECES = 8
 PIECE = ROWS // PIECES
 HALF = ROWS // 2
 PART = SHARD // 2
@@ -142,6 +142,41 @@
     def shard_rows(j):
         return pl.ds(pl.multiple_of(j * SHARD, 32), SHARD)
 
+    barrier = pltpu.get_barrier_semaphore()
+    expected = 0
+
+    def arrive(peer):
+        pl.semaphore_signal(barrier, inc=1, device_id=peer, device_id_type=MESH)
+
+    def answer(sem, peer):
+        pl.semaphore_signal(sem, inc=1, device_id=peer, device_id_type=MESH)
+
+    if WITH_FSDP:
+        for d in (1, 2, 3):
+            arrive(y_peer(d))
+        for d in (1, 2, 3):
+
+            @pl.when(z + d <= 3)
+            def _():
+                arrive(z_peer(lax.rem(z + d, 4)))
+
+        expected = expected + 3 + z
+    if WITH_REP:
+        for d in (1, 2, 3):
+
+            @pl.when(x + d <= 3)
+            def _():
+                arrive(x_peer(d))
+
+        @pl.when(zh == 0)
+        def _():
+            arrive(h_peer)
+
+        @pl.when(core == 1)
+        def _():
+            arrive(core_peer)
+
+        expected = expected + x + zh + (1 - core)
     copies = {}
     if WITH_FSDP:
         copies["tokens"] = local(tokens.at[0], tok_v, loc.at[0])
@@ -149,41 +184,6 @@
         copies["outer"] = local(outer, outer_v, loc.at[4])
         copies["inner"] = local(inner.at[0], inner_v, loc.at[6])
 
-    barrier = pltpu.get_barrier_semaphore()
-    expected = 0
-
-    def arrive(peer):
-        pl.semaphore_signal(barrier, inc=1, device_id=peer, device_id_type=MESH)
-
-    def answer(sem, peer):
-        pl.semaphore_signal(sem, inc=1, device_id=peer, device_id_type=MESH)
-
-    if WITH_FSDP:
-        for d in (1, 2, 3):
-            arrive(y_peer(d))
-        for d in (1, 2, 3):
-
-            @pl.when(z + d <= 3)
-            def _():
-                arrive(z_peer(lax.rem(z + d, 4)))
-
-        expected = expected + 3 + z
-    if WITH_REP:
-        for d in (1, 2, 3):
-
-            @pl.when(x + d <= 3)
-            def _():
-                arrive(x_peer(d))
-
-        @pl.when(zh == 0)
-        def _():
-            arrive(h_peer)
-
-        @pl.when(core == 1)
-        def _():
-            arrive(core_peer)
-
-        expected = expected + x + zh + (1 - core)
     pl.semaphore_wait(barrier, expected)
 
     def answers():
@@ -352,7 +352,7 @@
     def p_copy(piece, d):
         chunk = feature_chunk(NCHUNK - 1)
         to = lax.rem(y + d, 4)
-        rows = pl.ds(piece * PIECE, PIECE)
+        rows = pl.ds(pl.multiple_of(piece * PIECE, 16), PIECE)
         return remote(
             fx.at[chunk, to, rows], fin.at[y, chunk, rows], p_s.at[piece, d - 1], p_r.at[piece, d - 1], y_peer(d)
         )
@@ -424,13 +424,14 @@
 
     def features(step):
         chunk = feature_chunk(step)
-        product = lax.dot_general(
-            cx[...].reshape(4 * ROWS, KW),
-            wx[pl.ds(pl.multiple_of(chunk * CHUNK, CHUNK), CHUNK), :],
-            (((1,), (1,)), ((), ())),
-            preferred_element_type=F32,
-        )
-        fx[chunk] = product.astype(BF16).reshape(4, ROWS, CHUNK)
+        rows = pl.ds(pl.multiple_of(chunk * CHUNK, CHUNK), CHUNK)
+
+        def body(s, _):
+            product = lax.dot_general(cx[s], wx[rows, :], (((1,), (1,)), ((), ())), preferred_element_type=F32)
+            fx[chunk, s] = product.astype(BF16)
+            return 0
+
+        lax.fori_loop(0, 4, body, 0)
 
     def gain_part():
         gz[z] = jnp.zeros((16, LANE), F32)
@@ -481,6 +482,9 @@
         @pl.when(z > 0)
         def _():
             w_own(1).start()
+
+        for d in (1, 3, 2):
+            start(t_copy(0, d))
 
         answers()
 
@@ -506,9 +510,13 @@
     if WITH_REP:
         copies["outer"].wait()
         copies["inner"].wait()
-        for b in range(8):
-            lanes = slice(b * LANE, (b + 1) * LANE)
+
+        def differ(b, _):
+            lanes = pl.ds(pl.multiple_of(b * LANE, LANE), LANE)
             db[b] = outer_v[:, lanes] - inner_v[:, lanes].astype(F32)
+            return 0
+
+        lax.fori_loop(0, 8, differ, 0)
 
         @pl.when(core == 1)
         def _():
@@ -525,7 +533,7 @@
         start(c_copy(4))
         c_copy(1).wait_recv()
         start(c_copy(5))
-        for step in range(NCHUNK):
+        for step in range(1, NCHUNK):
             for d in (1, 3, 2):
                 start(t_copy(step, d))
 
@@ -570,10 +578,14 @@
         begin_sums(0)
         copies["w"].wait()
         weight_step(2)
-        for step in range(NCHUNK - 1):
+
+        def early_features(step, _):
             features(step)
             for d in (1, 3, 2):
-                start(f_copy(step, d))
+                f_copy(step, d).start()
+            return 0
+
+        lax.fori_loop(0, NCHUNK - 1, early_features, 0)
 
     if WITH_REP:
         h_copy().wait_recv()
@@ -597,19 +609,23 @@
     if WITH_FSDP:
         weight_step(3)
         features(NCHUNK - 1)
-        for piece in range(PIECES - 1):
+        for piece in range(PIECES):
             for d in (1, 3, 2):
                 start(p_copy(piece, d))
 
     if WITH_REP:
         copies["momentum"].wait()
         k_copy(1).wait_recv()
-        for b in range(8):
-            lanes = slice(b * LANE, (b + 1) * LANE)
+
+        def nesterov(b, _):
+            lanes = pl.ds(pl.multiple_of(b * LANE, LANE), LANE)
             pseudo = xs[b] / REPS
             momentum_next = MOMENTUM * mom_v[:, lanes] + pseudo
             nm_v[:, lanes] = momentum_next
             no_v[:, lanes] = outer_v[:, lanes] - OUTER_RATE * (pseudo + MOMENTUM * momentum_next)
+            return 0
+
+        lax.fori_loop(0, 8, nesterov, 0)
 
     if WITH_FSDP:
         own = local(fx.at[:, y], fin.at[y], loc.at[7])
@@ -635,31 +651,34 @@
         gy[y] = gz[0] + gz[1] + gz[2] + gz[3]
         for d in (1, 3, 2):
             start(gy_copy(d))
-        for d in (1, 3, 2):
-            start(p_copy(PIECES - 1, d))
         pass_sums(2, 1)
         own.wait()
         for step in range(NCHUNK - 1):
             for d in (1, 2, 3):
                 f_copy(step, d).wait_recv()
-        for piece in range(PIECES):
-            if piece == 1:
-                end_sums(0)
-            if piece == PIECES - 1:
-                end_sums(1)
-                for d in (1, 2, 3):
-                    gy_copy(d).wait_recv()
-                for b in range(4):
-                    for i in range(BLOCK // LANE):
-                        at = b * BLOCK + i * LANE
-                        gg_v[0:1, at : at + LANE] = gy[b, i : i + 1, :]
+
+        def last_rows(piece, _):
             for d in (1, 2, 3):
                 p_copy(piece, d).wait_recv()
             input_piece(piece)
+            return 0
+
+        end_sums(0)
+        lax.fori_loop(0, PIECES, last_rows, 0)
+        end_sums(1)
+        for d in (1, 2, 3):
+            gy_copy(d).wait_recv()
+        for b in range(4):
+            for i in range(BLOCK // LANE):
+                at = b * BLOCK + i * LANE
+                gg_v[0:1, at : at + LANE] = gy[b, i : i + 1, :]
 
     for copy in sends:
         copy.wait_send()
     if WITH_FSDP:
+        for step in range(NCHUNK - 1):
+            for d in (1, 2, 3):
+                f_copy(step, d).wait_send()
 
         @pl.when(z < 3)
         def _():

time: 80.8 us -> 80.1 us (level)
  no operation moved by 1% of the time
where the time goes in v4:
time: 80.1 us; the launch traced here: 79.2 us
  Pallas kernels  78.6 us (98%)
    pallas_call x1, Pallas kernels, call(): pl.pallas_call(kernel, out_shape=tuple((pltpu.VMEM(shape.shape, shape.dty...  76 us
    pallas_call x1, Pallas kernels, call(): pl.pallas_call(finish, out_shape=shapes, in_specs=[on_chip] * 5, out_spec...  2.62 us

profile of v4, /device:TPU:6, one launch (start us, length us, event | category | flops | bytes accessed | tf_op | source)
XLA Modules:
  0.0 79.2 jit_solution(17436999868153958839)
XLA Ops:
  0.6 76.0 %inner_outer_step.1 = (bf16[1,256,4608]{2,1,0:T(8,128)(2,1)S(1)}, f32[1,4608]{1,0:T(1,128)S(1)}, f32[1,288,1024]{2,1,0:T(8,128)S(1)}, f32[288,1024]{1,0:T(8,128)S(1)}, f32[288,1024]{1,0:T(8,128)S(1)}) custom-call(bf16[1,256,4608]{2,1,0:T(8,128)(2,1)} %tokens.1, f32[1,4608]{1,0:T(1,128)} %gain.1, bf16[1,288,1024]{2,1,0:T(8,128)(2,1)} %weight.1, ...), custom_call_target="tpu_custom_call" | custom-call | flops 4831838208 | bytes 16777216 | tf_op jit(solution)/shard_map/inner_outer_step/pallas_call | solution.py:792
  76.6 2.6 %write_results.1 = (bf16[1,256,4608]{2,1,0:T(8,128)(2,1)}, f32[1,4608]{1,0:T(1,128)}, f32[1,288,1024]{2,1,0:T(8,128)}, f32[288,1024]{1,0:T(8,128)}, f32[288,1024]{1,0:T(8,128)}) custom-call(bf16[1,256,4608]{2,1,0:T(8,128)(2,1)S(1)} %get-tuple-element.10.refs_0_, f32[1,4608]{1,0:T(1,128)S(1)} %get-tuple-element.11.refs_1_, ...), custom_call_target="tpu_custom_call" | custom-call | tf_op jit(solution)/shard_map/write_results/pallas_call | solution.py:806

commit v5 on v4

--- a/solution.py
+++ b/solution.py
@@ -26,10 +26,31 @@
 HALF = ROWS // 2
 PART = SHARD // 2
 LANE = 128
-VMEM_LIMIT = 48 * 2**20
+VMEM_LIMIT = 44 * 2**20
 
 WITH_FSDP = True
 WITH_REP = True
+
+
+def input_rows(fin, tok_v, rs_own, gain_v, first, target, to):
+    rows = pl.ds(first, 16)
+    root = rs_own[rows, :]
+
+    def terms(s, t, q):
+        at = s * BLOCK + t * CHUNK + q * LANE
+        grad = fin[s, t, rows, q * LANE : (q + 1) * LANE].astype(F32)
+        unit = tok_v[rows, at : at + LANE].astype(F32) * root
+        return at, grad * (1.0 + gain_v[0:1, at : at + LANE]), unit
+
+    places = [(s, t, q) for s in range(4) for t in range(NCHUNK) for q in range(CHUNK // LANE)]
+    total = jnp.zeros((16, LANE), F32)
+    for place in places:
+        _, scaled, unit = terms(*place)
+        total = total + scaled * unit
+    projected = jnp.sum(total, axis=1, keepdims=True) / D
+    for place in places:
+        at, scaled, unit = terms(*place)
+        target[pl.ds(to, 16), at : at + LANE] = (root * (scaled - unit * projected)).astype(BF16)
 
 
 def kernel(
@@ -41,16 +62,17 @@
     momentum,
     inner,
     ig_v,
-    gg_v,
     wg_v,
     no_v,
     nm_v,
+    fin,
     tok_v,
+    rs_own,
     gain_v,
+    gy,
     cx,
     wx,
     tx,
-    rs_own,
     rsx,
     rb,
     nt,
@@ -59,9 +81,7 @@
     ru,
     rd,
     fx,
-    fin,
     gz,
-    gy,
     outer_v,
     mom_v,
     inner_v,
@@ -453,24 +473,8 @@
 
     def input_piece(piece):
         def body(i, _):
-            rows = pl.ds(pl.multiple_of(piece * PIECE + i * 16, 16), 16)
-            root = rs_own[rows, :]
-
-            def terms(s, t, q):
-                at = s * BLOCK + t * CHUNK + q * LANE
-                grad = fin[s, t, rows, q * LANE : (q + 1) * LANE].astype(F32)
-                unit = tok_v[rows, at : at + LANE].astype(F32) * root
-                return at, grad * (1.0 + gain_v[0:1, at : at + LANE]), unit
-
-            places = [(s, t, q) for s in range(4) for t in range(NCHUNK) for q in range(CHUNK // LANE)]
-            total = jnp.zeros((16, LANE), F32)
-            for place in places:
-                _, scaled, unit = terms(*place)
-                total = total + scaled * unit
-            projected = jnp.sum(total, axis=1, keepdims=True) / D
-            for place in places:
-                at, scaled, unit = terms(*place)
-                ig_v[0, rows, at : at + LANE] = (root * (scaled - unit * projected)).astype(BF16)
+            at = pl.multiple_of(piece * PIECE + i * 16, 16)
+            input_rows(fin, tok_v, rs_own, gain_v, at, ig_v.at[0], at)
             return 0
 
         lax.fori_loop(0, PIECE // 16, body, 0)
@@ -609,7 +613,7 @@
     if WITH_FSDP:
         weight_step(3)
         features(NCHUNK - 1)
-        for piece in range(PIECES):
+        for piece in range(PIECES - 2):
             for d in (1, 3, 2):
                 start(p_copy(piece, d))
 
@@ -651,6 +655,9 @@
         gy[y] = gz[0] + gz[1] + gz[2] + gz[3]
         for d in (1, 3, 2):
             start(gy_copy(d))
+        for piece in range(PIECES - 2, PIECES):
+            for d in (1, 3, 2):
+                start(p_copy(piece, d))
         pass_sums(2, 1)
         own.wait()
         for step in range(NCHUNK - 1):
@@ -664,14 +671,12 @@
             return 0
 
         end_sums(0)
-        lax.fori_loop(0, PIECES, last_rows, 0)
+        lax.fori_loop(0, PIECES - 1, last_rows, 0)
+        for d in (1, 2, 3):
+            p_copy(PIECES - 1, d).wait_recv()
         end_sums(1)
         for d in (1, 2, 3):
             gy_copy(d).wait_recv()
-        for b in range(4):
-            for i in range(BLOCK // LANE):
-                at = b * BLOCK + i * LANE
-                gg_v[0:1, at : at + LANE] = gy[b, i : i + 1, :]
 
     for copy in sends:
         copy.wait_send()
@@ -703,14 +708,36 @@
                 g_up(lax.rem(z + d, 4), part).wait_send()
 
 
-def finish(*refs):
-    sources, targets, sems = refs[:5], refs[5:10], refs[10]
-    copies = [
-        pltpu.make_async_copy(source, target, sems.at[i])
-        for i, (source, target) in enumerate(zip(sources, targets))
+def finish(
+    ig_v, wg_v, no_v, nm_v, fin, tok_v, rs_own, gain_v, gy,
+    input_grad, gain_grad, weight_grad, new_outer, new_momentum,
+    last_v, gg_v, sems,
+):
+    done = ROWS - PIECE
+    pairs = [
+        (ig_v.at[0, pl.ds(0, done)], input_grad.at[0, pl.ds(0, done)]),
+        (wg_v, weight_grad),
+        (no_v, new_outer),
+        (nm_v, new_momentum),
+        (last_v, input_grad.at[0, pl.ds(done, PIECE)]),
+        (gg_v, gain_grad),
     ]
-    for copy in copies:
+    copies = [pltpu.make_async_copy(source, target, sems.at[i]) for i, (source, target) in enumerate(pairs)]
+    for copy in copies[:4]:
         copy.start()
+
+    def body(i, _):
+        at = pl.multiple_of(i * 16, 16)
+        input_rows(fin, tok_v, rs_own, gain_v, done + at, last_v, at)
+        return 0
+
+    lax.fori_loop(0, PIECE // 16, body, 0)
+    copies[4].start()
+    for b in range(4):
+        for i in range(BLOCK // LANE):
+            at = b * BLOCK + i * LANE
+            gg_v[0:1, at : at + LANE] = gy[b, i : i + 1, :]
+    copies[5].start()
     for copy in copies:
         copy.wait()
 
@@ -724,14 +751,22 @@
         jax.ShapeDtypeStruct((SHARD, KW), F32),
         jax.ShapeDtypeStruct((SHARD, KW), F32),
     )
+    held = (
+        pltpu.VMEM((1, ROWS, D), BF16),
+        pltpu.VMEM((1, SHARD, KW), F32),
+        pltpu.VMEM((SHARD, KW), F32),
+        pltpu.VMEM((SHARD, KW), F32),
+        pltpu.VMEM((4, NCHUNK, ROWS, CHUNK), BF16),
+        pltpu.VMEM((ROWS, D), BF16),
+        pltpu.VMEM((ROWS, LANE), F32),
+        pltpu.VMEM((1, D), F32),
+        pltpu.VMEM((4, 16, LANE), F32),
+    )
     dma = pltpu.SemaphoreType.DMA
     scratch = [
-        pltpu.VMEM((ROWS, D), BF16),
-        pltpu.VMEM((1, D), F32),
         pltpu.VMEM((4, ROWS, KW), BF16),
         pltpu.VMEM((BLOCK, KW), BF16),
         pltpu.VMEM((NCHUNK, 4, ROWS, CHUNK), BF16),
-        pltpu.VMEM((ROWS, LANE), F32),
         pltpu.VMEM((4, 8, ROWS), F32),
         pltpu.VMEM((4, ROWS, LANE), F32),
         pltpu.VMEM((4, CHUNK, ROWS), BF16),
@@ -740,8 +775,6 @@
         pltpu.VMEM((4, SHARD, KW), BF16),
         pltpu.VMEM((4, SHARD, KW), BF16),
         pltpu.VMEM((NCHUNK, 4, ROWS, CHUNK), BF16),
-        pltpu.VMEM((4, NCHUNK, ROWS, CHUNK), BF16),
-        pltpu.VMEM((4, 16, LANE), F32),
         pltpu.VMEM((4, 16, LANE), F32),
         pltpu.VMEM((SHARD, KW), F32),
         pltpu.VMEM((SHARD, KW), F32),
@@ -791,9 +824,9 @@
     on_chip = pl.BlockSpec(memory_space=pltpu.VMEM)
     results = pl.pallas_call(
         kernel,
-        out_shape=tuple(pltpu.VMEM(shape.shape, shape.dtype) for shape in shapes),
+        out_shape=held,
         in_specs=[anywhere] * 7,
-        out_specs=[on_chip] * 5,
+        out_specs=[on_chip] * len(held),
         scratch_shapes=scratch,
         compiler_params=pltpu.CompilerParams(
             collective_id=0, has_side_effects=True, vmem_limit_bytes=VMEM_LIMIT
@@ -806,10 +839,10 @@
     return pl.pallas_call(
         finish,
         out_shape=shapes,
-        in_specs=[on_chip] * 5,
+        in_specs=[on_chip] * len(held),
         out_specs=[anywhere] * 5,
-        scratch_shapes=[pltpu.SemaphoreType.DMA((5,))],
-        compiler_params=pltpu.CompilerParams(vmem_limit_bytes=2**20),
+        scratch_shapes=[pltpu.VMEM((PIECE, D), BF16), pltpu.VMEM((1, D), F32), pltpu.SemaphoreType.DMA((6,))],
+        compiler_params=pltpu.CompilerParams(vmem_limit_bytes=2**22),
         name="write_results",
     )(*(pltpu.with_memory_space_constraint(result, pltpu.VMEM) for result in results))
 

time: 80.1 us -> 80 us (level)
  no operation moved by 1% of the time
where the time goes in v5:
time: 80 us; the launch traced here: 79 us
  Pallas kernels  78.3 us (98%)
    pallas_call x1, Pallas kernels, call(): pl.pallas_call(kernel, out_shape=held, in_specs=[anywhere] * 7, out_specs...  75.7 us
    pallas_call x1, Pallas kernels, call(): pl.pallas_call(finish, out_shape=shapes, in_specs=[on_chip] * len(held),...  2.58 us

profile of v5, /device:TPU:6, one launch (start us, length us, event | category | flops | bytes accessed | tf_op | source)
XLA Modules:
  0.0 79.0 jit_solution(7346608432249367106)
XLA Ops:
  0.6 75.7 %inner_outer_step.1 = (bf16[1,256,4608]{2,1,0:T(8,128)(2,1)S(1)}, f32[1,288,1024]{2,1,0:T(8,128)S(1)}, f32[288,1024]{1,0:T(8,128)S(1)}, f32[288,1024]{1,0:T(8,12...) custom-call(bf16[1,256,4608]{2,1,0:T(8,128)(2,1)} %tokens.1, ...), custom_call_target="tpu_custom_call" | custom-call | flops 4831838208 | bytes 16777216 | tf_op jit(solution)/shard_map/inner_outer_step/pallas_call | solution.py:825
  76.4 2.6 %write_results.1 = (bf16[1,256,4608]{2,1,0:T(8,128)(2,1)}, f32[1,4608]{1,0:T(1,128)}, f32[1,288,1024]{2,1,0:T(8,128)}, f32[288,1024]{1,0:T(8,128)}, f32[288,1024]{1,0:T(8,128)}) custom-call(bf16[1,256,4608]{2,1,0:T(8,128)(2,1)S(1)} %get-tuple-element.14.ig_v, f32[1,288,1024]{2,1,0:T(8,128)S(1)} %get-tuple-element.15.wg_v, ...), custom_call_target="tpu_custom_call" | custom-call | tf_op jit(solution)/shard_map/write_results/pallas_call | solution.py:839
